TPU v7x, 256 devices: a whole 4x4x8 slice. The times are simulated.
256 devices in a mesh: seq: 32 (over x, z), head: 8 (over y, core).
Axes of the slice: x: 4, y: 4, z: 8, core: 2. Of those that a mesh axis runs over, the one named last changes fastest.
Arguments:
- queries: bfloat16 [32768, 5120], P('seq', 'head')
- keys: bfloat16 [32768, 5120], P('seq', 'head')
- values: bfloat16 [32768, 5120], P('seq', 'head'), may hold values from -6 to 6
- query_gain: float32 [5120], P('head'), may hold values from 0.1 to 1.9
- key_gain: float32 [5120], P('head'), may hold values from 0.1 to 1.9
- shapes: int32 [8, 3], replicated, may hold values from 4 to 32, as said below
- windows: int32 [256, 27], P('seq'), may hold values from -1 to 255, as said below
- text_keys: bfloat16 [32, 256, 5120], P(None, 'seq', 'head')
- text_values: bfloat16 [32, 256, 5120], P(None, 'seq', 'head'), may hold values from -6 to 6
- owner: int32 [8], replicated, may hold values from 0 to 31, as said below
Outputs:
- attended: bfloat16 [32768, 5120], P('seq', 'head')
Inputs may be any that keep to these rules, and one draw needn't show every extreme that they name: `shapes`: row s is (frames, height, width) of video s in tokens: height and width are 16 and 32, or 32 and 16, so a frame has 4 tiles; each video has from 16 to 48 tiles, and the videos' tiles add up to 256, so no tile holds tokens of two videos. `windows`: entry k of row g stands for the tile k // 9 - 1 frames, (k // 3) % 3 - 1 tile rows and k % 3 - 1 tile columns away from tile g in its video: it holds that tile's number or -1; it is -1 wherever that tile lies outside the video, and entry 13 is always g. `owner`: no two videos share a panel.
All inputs are finite; a program needn't handle non-finite values.
Results may differ from a plain program's by a relative error of at most 0.012.
Values may be sent and summed in bfloat16 or wider, within the bound.
A program may use at most 128 MiB of HBM per device.

v0:
```python
import jax
import jax.numpy as jnp
from jax import lax
from jax.sharding import PartitionSpec as P

HEAD_DIM = 128
D = 5120
TILE_H = 8
TILE_W = 16
REACH = 7
TXT = 256


epsilon = 1e-06


def extended_2(cells, sides, width):
    for axis, dim in sides:
        count = lax.axis_size(axis)
        ends = count - 1
        head = lax.slice_in_dim(cells, 0, width, axis=dim)
        tail = lax.slice_in_dim(cells, cells.shape[dim] - width, cells.shape[dim], axis=dim)
        cells = jnp.concatenate(
            [
                lax.ppermute(tail, axis, [(i, (i + 1) % count) for i in range(ends)]),
                cells,
                lax.ppermute(head, axis, [((i + 1) % count, i) for i in range(ends)]),
            ],
            axis=dim,
        )
    return cells


def tile_table(shape_rows):
    per_frame = shape_rows[:, 1] // TILE_H * (shape_rows[:, 2] // TILE_W)
    tile_counts = shape_rows[:, 0] * per_frame
    tile_ends = jnp.cumsum(tile_counts)
    return (tile_ends - tile_counts, tile_ends)


def locate(tile_ids, shape_rows, tile_starts, tile_ends):
    sample_ids = jnp.sum((tile_ids[:, None] >= tile_ends[None, :]).astype(jnp.int32), axis=1)
    one_hot = (
        sample_ids[:, None] == jnp.arange(tile_ends.shape[0], dtype=jnp.int32)[None, :]
    ).astype(jnp.int32)
    first_tiles = jnp.sum(one_hot * tile_starts[None, :], axis=1)
    row_counts = jnp.sum(one_hot * (shape_rows[:, 1] // TILE_H)[None, :], axis=1)
    col_counts = jnp.sum(one_hot * (shape_rows[:, 2] // TILE_W)[None, :], axis=1)
    offsets = tile_ids - first_tiles
    per_frame = row_counts * col_counts
    within = offsets % per_frame
    return (sample_ids, one_hot, offsets // per_frame, within // col_counts, within % col_counts)


def rope_angles(frames, bands, columns, head_size):
    inner = jnp.arange(TILE_H * TILE_W, dtype=jnp.int32)
    tile_total = frames.shape[0]
    time_pos = (
        jnp.broadcast_to(frames[:, None], (tile_total, inner.shape[0]))
        .reshape(-1)
        .astype(jnp.float32)
    )
    row_pos = (bands[:, None] * TILE_H + inner[None, :] // TILE_W).reshape(-1).astype(jnp.float32)
    col_pos = (columns[:, None] * TILE_W + inner[None, :] % TILE_W).reshape(-1).astype(jnp.float32)
    third = head_size // 6
    part_sizes = (head_size - 4 * third, 2 * third, 2 * third)
    angle_parts = []
    for position, part_size in zip((time_pos, row_pos, col_pos), part_sizes):
        frequency = 10000.0 ** (-jnp.arange(0, part_size, 2, dtype=jnp.float32) / part_size)
        angle_parts.append(position[:, None] * frequency[None, :])
    return jnp.concatenate(angle_parts, axis=1)


def rotate(field, angles):
    paired = field.reshape(field.shape[0], field.shape[1], field.shape[2] // 2, 2)
    cosine = jnp.cos(angles)[:, None, :]
    sine = jnp.sin(angles)[:, None, :]
    even_part = paired[..., 0]
    odd_part = paired[..., 1]
    turned = jnp.stack(
        [even_part * cosine - odd_part * sine, even_part * sine + odd_part * cosine], axis=-1
    )
    return turned.reshape(field.shape)


def finish_rows(widened, squares, gain, angles, head_count):
    scaled = widened * lax.rsqrt(squares / D + epsilon)[:, None] * gain[None, :]
    turned = rotate(scaled.reshape(widened.shape[0], head_count, HEAD_DIM), angles)
    return turned.reshape(widened.shape).astype(jnp.bfloat16)


def local(
    queries, keys, values, query_gain, key_gain, shapes, windows, text_keys, text_values, owner
):
    row_count, feat_width = queries.shape
    head_count = feat_width // HEAD_DIM
    tile_rows = TILE_H * TILE_W
    tiles_here = row_count // tile_rows
    first_global = lax.axis_index("seq") * tiles_here
    tile_starts, tile_ends = tile_table(shapes)
    tile_ids = first_global + jnp.arange(tiles_here, dtype=jnp.int32)
    sample_ids, one_hot, frames, bands, columns = locate(tile_ids, shapes, tile_starts, tile_ends)
    angles = rope_angles(frames, bands, columns, HEAD_DIM)
    query_wide = queries.astype(jnp.float32)
    key_wide = keys.astype(jnp.float32)
    query_squares, key_squares = lax.psum(
        (jnp.sum(query_wide * query_wide, axis=1), jnp.sum(key_wide * key_wide, axis=1)), "head"
    )
    q_hat = finish_rows(query_wide, query_squares, query_gain, angles, head_count)
    k_hat = finish_rows(key_wide, key_squares, key_gain, angles, head_count)
    key_value = jnp.stack([k_hat, values])
    extended = extended_2(key_value, (("seq", 1),), REACH * tile_rows)
    panel_of_tile = jnp.sum(one_hot * owner[None, :], axis=1)
    prompt_pair = jnp.stack([text_keys, text_values])
    every_panel = lax.all_gather(prompt_pair, "seq", axis=2, tiled=True)
    wanted = jnp.stack([panel_of_tile[0], panel_of_tile[tiles_here - 1]])
    panels = jnp.take(every_panel, wanted, axis=1)
    prompt_keys = panels[0].reshape(2 * TXT, head_count, HEAD_DIM)
    prompt_values = panels[1].reshape(2 * TXT, head_count, HEAD_DIM)
    second_slot = (sample_ids != sample_ids[0]).astype(jnp.int32)
    prompt_allowed = second_slot[:, None] == (jnp.arange(2 * TXT, dtype=jnp.int32) // TXT)[None, :]
    key_tiles = first_global - REACH + jnp.arange(tiles_here + 2 * REACH, dtype=jnp.int32)
    window_allowed = (
        jnp.any(windows[:, :, None] == key_tiles[None, None, :], axis=1) & (key_tiles >= 0)[None, :]
    )
    group_tiles = 4
    span_tiles = group_tiles + 2 * REACH
    group_rows = group_tiles * tile_rows
    factor = HEAD_DIM ** (-0.5)

    def attend(block_index):
        start_tile = block_index * group_tiles
        query_rows = lax.dynamic_slice_in_dim(q_hat, start_tile * tile_rows, group_rows, 0).reshape(
            group_rows, head_count, HEAD_DIM
        )
        key_rows = lax.dynamic_slice_in_dim(
            extended[0], start_tile * tile_rows, span_tiles * tile_rows, 0
        ).reshape(span_tiles * tile_rows, head_count, HEAD_DIM)
        value_rows = lax.dynamic_slice_in_dim(
            extended[1], start_tile * tile_rows, span_tiles * tile_rows, 0
        ).reshape(span_tiles * tile_rows, head_count, HEAD_DIM)
        allowed = lax.dynamic_slice(
            window_allowed, (start_tile, start_tile), (group_tiles, span_tiles)
        )
        prompt_ok = lax.dynamic_slice_in_dim(prompt_allowed, start_tile, group_tiles, 0)
        key_mask = jnp.concatenate(
            [
                jnp.repeat(jnp.repeat(allowed, tile_rows, axis=0), tile_rows, axis=1),
                jnp.repeat(prompt_ok, tile_rows, axis=0),
            ],
            axis=1,
        )
        all_keys = jnp.concatenate([key_rows, prompt_keys], axis=0)
        all_values = jnp.concatenate([value_rows, prompt_values], axis=0)
        scores = (
            jnp.einsum("qhd,khd->hqk", query_rows, all_keys, preferred_element_type=jnp.float32)
            * factor
        )
        scores = jnp.where(key_mask[None, :, :], scores, -jnp.inf)
        largest = jnp.max(scores, axis=-1, keepdims=True)
        weights = jnp.exp(scores - largest)
        totals = jnp.sum(weights, axis=-1)
        mixed = jnp.einsum(
            "hqk,khd->qhd",
            weights.astype(jnp.bfloat16),
            all_values,
            preferred_element_type=jnp.float32,
        )
        mixed = mixed / jnp.transpose(totals)[:, :, None]
        return mixed.astype(jnp.bfloat16).reshape(group_rows, feat_width)

    outputs = lax.map(attend, jnp.arange(tiles_here // group_tiles, dtype=jnp.int32))
    return outputs.reshape(row_count, feat_width)


def solution(mesh):
    placed = (
        P("seq", "head"),
        P("seq", "head"),
        P("seq", "head"),
        P("head"),
        P("head"),
        P(),
        P("seq", None),
        P(None, "seq", "head"),
        P(None, "seq", "head"),
        P(),
    )
    return jax.shard_map(
        local, mesh=mesh, in_specs=placed, out_specs=P("seq", "head"), check_vma=False
    )
```

profile of v0, /device:TPU:1, one launch (start us, length us, event | category | flops | bytes accessed | tf_op | source)
XLA Modules:
  0.0 367.0 jit_solution(5512880522823748688)
XLA Ops:
  6.5 2.1 pad_maximum_fusion.4
  8.7 0.3 fusion.26
  9.1 0.3 fusion.28
  9.4 15.2 %all-reduce = (f32[1024]{0:T(1024)S(1)}, f32[1024]{0:T(1024)S(1)}) all-reduce(f32[1024]{0:T(1024)S(1)} %fusion.26, f32[1024]{0:T(1024)S(1)} %fusion.28), channel_id=1, replica_groups=mesh['seq'=32,'head'=8] {'head'}, use_global_device_ids=true, to_apply=%region_8.9 | all-reduce | flops 2048 | bytes 16384 | tf_op jit(solution)/shard_map/psum | solution.py:106
  24.6 1.7 fusion.27
  26.3 2.1 copy.28
  28.5 4.5 %reshape_reshape.8 = f32[1024,5,64,2]{0,3,2,1:T(2,128)} reshape(f32[1024,640]{0,1:T(8,128)} %copy.28) | data formatting | bytes 5242880 | tf_op jit(solution)/shard_map/reshape;reshape | solution.py:75
  33.0 1.6 fusion.29
  34.6 2.1 copy.31
  36.7 4.6 %reshape_reshape.9 = f32[1024,5,64,2]{0,3,2,1:T(2,128)} reshape(f32[1024,640]{0,1:T(8,128)} %copy.31) | data formatting | bytes 5242880 | tf_op jit(solution)/shard_map/reshape;reshape | solution.py:75
  41.8 0.2 select_reduce_fusion
  42.0 0.3 fusion.39
  42.7 1.0 fusion.32
  43.7 9.1 %subtract_convert_fusion = (bf16[1024,5,64,1]{0,3,2,1:T(2,128)(2,1)}, bf16[1024,5,64,1]{0,3,2,1:T(2,128)(2,1)}, bf16[1024,5,64,1]{0,3,2,1:T(2,128)(2,1)S(1)}, bf16[1024,5,64,1]{0,3,2,1:T(2,128)(2,1)S(1)}) fusion(f32[1024,5,64,2]{0,3,2,1:T(2,128)} %reshape_reshape.9, f32[1024,64]{0,1:T(8,128)S(1)} %get-tuple-element.183, ...), kind=kLoop, calls=%fused_computation.46 | loop fusion | flops 5242880 | bytes 8388608 | tf_op jit(solution)/shard_map/convert.2
  52.8 3.0 pad_maximum_fusion.2
  55.8 0.5 convert_element_type.83
  56.3 1.6 copy.29
  58.0 2.4 fusion.30
  60.4 3.4 collective-permute-start
  63.8 1.5 collective-permute-start.1
  65.3 5.8 %pad_maximum_fusion.3 = bf16[1024,5,64,2]{0,3,2,1:T(2,128)(2,1)} fusion(bf16[1024,5,64,1]{0,3,2,1:T(2,128)(2,1)} %get-tuple-element.173, bf16[1024,5,64,1]{0,3,2,1:T(2,128)(2,1)} %get-tuple-element.172), kind=kLoop, calls=%fused_computation.43 | loop fusion | flops 2621440 | bytes 2621440 | tf_op jit(solution)/shard_map/stack | solution.py:80
  71.0 4.1 %convert_element_type.86 = bf16[1024,640]{0,1:T(8,128)(2,1)} reshape(bf16[1024,5,64,2]{0,3,2,1:T(2,128)(2,1)} %pad_maximum_fusion.3) | data formatting | bytes 2621440 | tf_op jit(solution)/shard_map/convert_element_type | solution.py:89
  75.2 0.7 fusion.43
  75.9 1.3 compare_and_fusion
  77.2 1.3 fusion.36
  78.5 0.5 compare_reduce_fusion
  79.3 68.9 %collective-permute-done = bf16[2,896,640]{1,2,0:T(8,128)(2,1)} collective-permute-done((bf16[2,896,640]{1,2,0:T(8,128)(2,1)}, bf16[2,896,640]{1,2,0:T(8,128)(2,1)}, u32[]{:S(2)}, u32[]{:S(2)}) %collective-permute-start) | collective-permute-done | bytes 2293792 | tf_op jit(solution)/shard_map/ppermute | solution.py:25
  148.2 10.7 %collective-permute-done.1 = bf16[2,896,640]{1,2,0:T(8,128)(2,1)} collective-permute-done((bf16[2,896,640]{1,2,0:T(8,128)(2,1)}, bf16[2,896,640]{1,2,0:T(8,128)(2,1)}, u32[]{:S(2)}, u32[]{:S(2)}) %collective-permute-start.1) | collective-permute-done | bytes 2293792 | tf_op jit(solution)/shard_map/ppermute | solution.py:27
  158.9 5.7 %pad_maximum_fusion = bf16[2,2816,640]{1,2,0:T(8,128)(2,1)} fusion(bf16[2,896,640]{1,2,0:T(8,128)(2,1)} %collective-permute-done.1, bf16[1,1024,640]{1,2,0:T(8,128)(2,1)S(1)} %bitcast.119, bf16[1,1024,640]{1,2,0:T(8,128)(2,1)S(1)} %convert_element_type.83, bf16[2,896,640]{1,2,0:T(8,128)(2,1)} %collective-permute-done), kind=kLoop, calls=%fused_computation.29 | loop fusion | flops 28835840 | bytes 14417920 | tf_op jit(solution)/shard_map/concatenate | solution.py:23
  164.6 58.4 %all-gather.2.cloned.1.call-done = bf16[2,32,256,640]{3,2,1,0:T(8,128)(2,1)} async-done(((bf16[2,32,8,640]{3,2,1,0:T(8,128)(2,1)}), bf16[2,32,256,640]{3,2,1,0:T(8,128)(2,1)}) %all-gather.2.cloned.1.call-update) | async-done | bytes 20971536 | tf_op jit(solution)/shard_map/all_gather | solution.py:115
  223.0 7.7 %gather_fusion = bf16[2,2,256,640]{3,2,1,0:T(8,128)(2,1)S(1)} fusion(bf16[2,32,256,640]{3,2,1,0:T(8,128)(2,1)} %all-gather.2.cloned.1.call-done, s32[1024]{0:T(1024)S(1)} %pad_clamp_fusion), kind=kCustom, calls=%fused_computation | custom fusion | bytes 2621448 | tf_op jit(solution)/shard_map/jit(_take)/gather | solution.py:117
  231.1 0.7 reshape.554
  231.8 0.9 copy.33
  232.8 0.9 copy.30
  233.7 1.2 reshape_squeeze.6
  235.0 125.1 %while.12 = (s32[]{:T(128)}, bf16[2,512,640]{2,1,0:T(8,128)(2,1)}, bf16[2,2816,640]{1,2,0:T(8,128)(2,1)}, s32[2]{0:T(128)S(1)}, bf16[512,5,128]{0,2,1:T(8,128)(2...) while((s32[]{:T(128)}, bf16[2,512,640]{2,1,0:T(8,128)(2,1)}, ...), condition=%wide.region_14.15_spmd, body=%wide.region_11.14_spmd.sunk | while | flops 3786796032 | bytes 151642208 | solution.py:172
  235.0 0.7 dynamic_slice.43
  236.6 0.3 broadcast_in_dim.137
  237.0 1.6 broadcast_in_dim.136
  238.8 0.5 pad_add_fusion.2
  239.3 3.2 copy.51
  243.2 3.6 fusion.54
  246.8 2.0 constant_dynamic-slice_fusion.9
  248.8 3.3 copy.52
  252.2 1.1 constant_dynamic-slice_fusion.8
  253.3 15.2 %fusion.55 = (f32[5,512]{1,0:T(8,128)S(1)}, f32[5,512,2816]{2,1,0:T(8,128)}) fusion(pred[512,2816]{1,0:T(8,128)(4,1)} %copy.51, bf16[512,5,128]{0,2,1:T(8,128)(2,1)S(1)} %bitcast.117, bf16[512,5,128]{2,0,1:T(8,128)(2,1)} %get-tuple-element.304, bf16[2304,5,128]{2,0,1:T(8,128)(2,1)} %copy.52), kind=kOutput, calls=%fused_computation.3.clone.1 | convolution fusion | flops 1874327040 | bytes 34547712 | tf_op jit(solution)/shard_map/while/body/eval_jaxpr/qhd,khd->hqk/dot_general | solution.py:156
  268.5 13.8 %fusion.56 = f32[5,512]{1,0:T(8,128)S(1)} fusion(f32[5,512,2816]{2,1,0:T(8,128)} %get-tuple-element.257, f32[5,512]{1,0:T(8,128)S(1)} %get-tuple-element.258, pred[512,2816]{1,0:T(8,128)(4,1)S(1)} %copy-done), kind=kLoop, calls=%fused_computation.4.clone.1 | loop fusion | flops 28833280 | bytes 30298112 | tf_op jit(solution)/shard_map/while/body/eval_jaxpr/reduce_sum | solution.py:162
  282.3 14.1 %divide_convert_fusion.2 = bf16[512,5,128]{0,2,1:T(8,128)(2,1)S(1)} fusion(f32[512,5]{0,1:T(8,128)S(1)} %bitcast.122, f32[5,512,2816]{2,1,0:T(8,128)} %get-tuple-element.257, f32[5,512]{1,0:T(8,128)S(1)} %get-tuple-element.258, pred[512,2816]{1,0:T(8,128)(4,1)S(1)} %copy-done, bf16[512,5,128]{0,2,1:T(8,128)(2,1)S(1)} %copy-done.4, ...), kind=kOutput, calls=%fused_computation.17.clone.1 | convolution fusion | flops 1882193920 | bytes 34557952 | tf_op jit(solution)/shard_map/while/body/eval_jaxpr/hqk,khd->qhd/dot_general | solution.py:163
  296.4 0.3 copy.53
  296.7 0.9 constant_dynamic-update-slice_fusion.2
  297.6 0.7 dynamic_slice.43
  299.1 0.3 broadcast_in_dim.137
  299.6 1.6 broadcast_in_dim.136
  301.3 0.5 pad_add_fusion.2
  301.8 3.2 copy.51
  305.8 3.6 fusion.54
  309.4 2.0 constant_dynamic-slice_fusion.9
  311.4 3.3 copy.52
  314.7 1.1 constant_dynamic-slice_fusion.8
  315.9 15.2 %fusion.55 = (f32[5,512]{1,0:T(8,128)S(1)}, f32[5,512,2816]{2,1,0:T(8,128)}) fusion(pred[512,2816]{1,0:T(8,128)(4,1)} %copy.51, bf16[512,5,128]{0,2,1:T(8,128)(2,1)S(1)} %bitcast.117, bf16[512,5,128]{2,0,1:T(8,128)(2,1)} %get-tuple-element.304, bf16[2304,5,128]{2,0,1:T(8,128)(2,1)} %copy.52), kind=kOutput, calls=%fused_computation.3.clone.1 | convolution fusion | flops 1874327040 | bytes 34547712 | tf_op jit(solution)/shard_map/while/body/eval_jaxpr/qhd,khd->hqk/dot_general | solution.py:156
  331.1 13.8 %fusion.56 = f32[5,512]{1,0:T(8,128)S(1)} fusion(f32[5,512,2816]{2,1,0:T(8,128)} %get-tuple-element.257, f32[5,512]{1,0:T(8,128)S(1)} %get-tuple-element.258, pred[512,2816]{1,0:T(8,128)(4,1)S(1)} %copy-done), kind=kLoop, calls=%fused_computation.4.clone.1 | loop fusion | flops 28833280 | bytes 30298112 | tf_op jit(solution)/shard_map/while/body/eval_jaxpr/reduce_sum | solution.py:162
  344.8 14.1 %divide_convert_fusion.2 = bf16[512,5,128]{0,2,1:T(8,128)(2,1)S(1)} fusion(f32[512,5]{0,1:T(8,128)S(1)} %bitcast.122, f32[5,512,2816]{2,1,0:T(8,128)} %get-tuple-element.257, f32[5,512]{1,0:T(8,128)S(1)} %get-tuple-element.258, pred[512,2816]{1,0:T(8,128)(4,1)S(1)} %copy-done, bf16[512,5,128]{0,2,1:T(8,128)(2,1)S(1)} %copy-done.4, ...), kind=kOutput, calls=%fused_computation.17.clone.1 | convolution fusion | flops 1882193920 | bytes 34557952 | tf_op jit(solution)/shard_map/while/body/eval_jaxpr/hqk,khd->qhd/dot_general | solution.py:163
  358.9 0.3 copy.53
  359.2 0.9 constant_dynamic-update-slice_fusion.2
  (64 shorter events, 2.5 us)
Async XLA Ops:
  6.5 2.2 copy-start.2
  6.5 2.5 copy-start.3
  6.5 18.1 %copy-start.7 = (f32[640]{0:T(1024)S(1)}, f32[640]{0:T(1024)}, u32[]{:S(2)}) copy-start(f32[640]{0:T(1024)} %param.16) | copy-start | bytes 7684
  6.5 216.5 %all-gather.2.cloned.1.call-start = ((), (), s32[]{:S(2)}) async-start(), calls=%async_computation | async-start | bytes 21626880 | tf_op jit(solution)/shard_map/all_gather | solution.py:115
  28.5 4.5 %copy-start.8 = (f32[640]{0:T(1024)S(1)}, f32[640]{0:T(1024)}, u32[]{:S(2)}) copy-start(f32[640]{0:T(1024)} %param.15) | copy-start | bytes 7684
  36.7 4.6 %copy-start.5 = (s32[8,3]{0,1:T(4,128)S(1)}, s32[8,3]{0,1:T(4,128)}, u32[]{:S(2)}) copy-start(s32[8,3]{0,1:T(4,128)} %param.17) | copy-start | bytes 292
  36.7 5.0 %copy-start.9 = (s32[8]{0:T(128)S(1)}, s32[8]{0:T(128)}, u32[]{:S(2)}) copy-start(s32[8]{0:T(128)} %param.21) | copy-start | bytes 100
  36.7 7.0 %copy-start.1 = (f32[1024,5,64,2]{0,3,2,1:T(2,128)S(1)}, f32[1024,5,64,2]{0,3,2,1:T(2,128)}, u32[]{:S(2)}) copy-start(f32[1024,5,64,2]{0,3,2,1:T(2,128)} %reshape_reshape.8) | copy-start | bytes 7864324
  60.4 87.8 %collective-permute-start = (bf16[2,896,640]{1,2,0:T(8,128)(2,1)}, bf16[2,896,640]{1,2,0:T(8,128)(2,1)}, u32[]{:S(2)}, u32[]{:S(2)}) collective-permute-start(bf16[2,896,640]{1,2,0:T(8,128)(2,1)} %get-tuple-element.176), channel_id=1, source_target_pairs={{0,8},{8,16},{16,24},{24,32},{32,40},{40,48},{48,56},{56,64},{64,7... | collective-permute-start | bytes 6881288 | tf_op jit(solution)/shard_map/ppermute | solution.py:25
  63.8 95.1 %collective-permute-start.1 = (bf16[2,896,640]{1,2,0:T(8,128)(2,1)}, bf16[2,896,640]{1,2,0:T(8,128)(2,1)}, u32[]{:S(2)}, u32[]{:S(2)}) collective-permute-start(bf16[2,896,640]{1,2,0:T(8,128)(2,1)} %get-tuple-element.177), channel_id=1, source_target_pairs={{8,0},{16,8},{24,16},{32,24},{40,32},{48,40},{56,48},{64,56},{72,6... | collective-permute-start | bytes 6881288 | tf_op jit(solution)/shard_map/ppermute | solution.py:27
  65.3 13.2 %copy-start.6 = (s32[8,27]{1,0:T(8,128)S(1)}, s32[8,27]{1,0:T(8,128)}, u32[]{:S(2)}) copy-start(s32[8,27]{1,0:T(8,128)} %param.18) | copy-start | bytes 2596
  253.3 15.2 %copy-start = (pred[512,2816]{1,0:T(8,128)(4,1)S(1)}, pred[512,2816]{1,0:T(8,128)(4,1)}, u32[]{:S(2)}) copy-start(pred[512,2816]{1,0:T(8,128)(4,1)} %copy.51) | copy-start | bytes 4325380 | tf_op jit(solution)/shard_map/while
  268.5 13.8 %copy-start.4 = (bf16[512,5,128]{0,2,1:T(8,128)(2,1)S(1)}, bf16[512,5,128]{0,2,1:T(8,128)(2,1)}, u32[]{:S(2)}) copy-start(bf16[512,5,128]{0,2,1:T(8,128)(2,1)} %get-tuple-element.300) | copy-start | bytes 1966084 | tf_op jit(solution)/shard_map/while
  315.9 15.2 %copy-start = (pred[512,2816]{1,0:T(8,128)(4,1)S(1)}, pred[512,2816]{1,0:T(8,128)(4,1)}, u32[]{:S(2)}) copy-start(pred[512,2816]{1,0:T(8,128)(4,1)} %copy.51) | copy-start | bytes 4325380 | tf_op jit(solution)/shard_map/while
  331.1 13.8 %copy-start.4 = (bf16[512,5,128]{0,2,1:T(8,128)(2,1)S(1)}, bf16[512,5,128]{0,2,1:T(8,128)(2,1)}, u32[]{:S(2)}) copy-start(bf16[512,5,128]{0,2,1:T(8,128)(2,1)} %get-tuple-element.300) | copy-start | bytes 1966084 | tf_op jit(solution)/shard_map/while
Sparse Core Ops, SparseCore 0:
  10.1 212.9 all-gather.1
where the time goes:
time: 368 us; the launch traced here: 367 us
  waiting for transfers between devices  138 us (38%)
  local copies, waits for them, and re-layouts  67.2 us (18%)
  other arithmetic  66.5 us (18%)
  matrix products  58.5 us (16%)
  blocking collectives  15.2 us (4%)
  between operations  13.6 us (4%)
  starting transfers between devices  4.88 us (1%)
    ppermute x1, waiting for transfers between devices, extended_2(): lax.ppermute(tail, axis, [(i, (i + 1) % count) for i in range(ends)])  68.9 us
    all_gather x1, waiting for transfers between devices, local(): every_panel = lax.all_gather(prompt_pair, 'seq', axis=2, tiled=True)  58.4 us
    dot_general x2, matrix products, attend(): jnp.einsum('qhd,khd->hqk', query_rows, all_keys, preferred_element_type=j...  30.4 us
    dot_general x2, matrix products, attend(): jnp.einsum('hqk,khd->qhd', weights.astype(jnp.bfloat16), all_values, pref...  28.1 us
    reduce_sum x2, other arithmetic, attend(): totals = jnp.sum(weights, axis=-1)  27.5 us
    psum x1, blocking collectives, local(): lax.psum((jnp.sum(query_wide * query_wide, axis=1), jnp.sum(key_wide * ke...  15.2 us
    ppermute x1, waiting for transfers between devices, extended_2(): lax.ppermute(head, axis, [((i + 1) % count, i) for i in range(ends)])  10.7 us
    another operation x2, other arithmetic  9.31 us
  transfers between devices with their start and end apart: 3, of which 3 were waited for; matrix products, arithmetic and copies ran while one was open for 15% of the time, Pallas kernels for 0%

commit v1 on v0

v1 whole, which is shorter than its diff:
```python
import functools

import jax
import jax.numpy as jnp
import numpy as np
from jax import lax
from jax.experimental import pallas as pl
from jax.experimental.pallas import tpu as pltpu
from jax.sharding import PartitionSpec as P

HEAD_DIM = 128
D = 5120
TILE = 128
TXT = 256
SAMPLES = 8
NX, NZ = 4, 8
NSEQ = NX * NZ
NHEAD = 8
LH = 5
FRAME = 512
ROWS = 1024
WIDTH = LH * HEAD_DIM
PIECE = 8
EPSILON = 1e-06
SCALE = float(HEAD_DIM**-0.5 * np.log2(np.e))
MESH = pl.DeviceIdType.MESH
F32 = jnp.float32
BF16 = jnp.bfloat16
NEG = float("-inf")
T_ROW, R_ROW, C_ROW, TAB = 0, 16, 48, 80


def position_tables():
    third = HEAD_DIM // 6
    parts = (HEAD_DIM - 4 * third, 2 * third, 2 * third)
    counts = (16, 32, 32)
    tables = np.zeros((2, TAB, HEAD_DIM), np.float64)
    row, lane = 0, 0
    for part, count in zip(parts, counts):
        frequency = 10000.0 ** (-np.arange(0, part, 2, dtype=np.float64) / part)
        angle = np.repeat(np.arange(count)[:, None] * frequency[None, :], 2, axis=1)
        tables[0, row : row + count, lane : lane + part] = np.cos(angle)
        tables[1, row : row + count, lane : lane + part] = np.sin(angle)
        row, lane = row + count, lane + part
    return tables.astype(np.float32)


def nt(a, b):
    return lax.dot_general(a, b, (((1,), (1,)), ((), ())), preferred_element_type=F32)


def nn(a, b):
    return jnp.dot(a, b, preferred_element_type=F32)


def kernel(
    q_hbm, k_hbm, v_hbm, qg_ref, kg_ref, shapes_s, win_s, owner_s, tk_hbm, tv_hbm, tab_ref,
    out_hbm,
    qraw, kraw, vv, tkb, tvb, qh, kh, khl, vhl, gat, xs, pb, sums, coss, sins, rk, acc, ms, ls, outb, bias_s,
    loc_sem, out_sem, g_send, g_recv, v_send, v_recv, k_send, k_recv, s_send, s_recv, x_send, x_recv,
):
    me_s = lax.axis_index("seq")
    me_h = lax.axis_index("head")
    x, z = me_s // NZ, me_s % NZ

    def seq_dev(s):
        return (s, me_h)

    ring_r = seq_dev(x * NZ + (z + 1) % NZ)
    ring_l = seq_dev(x * NZ + (z + NZ - 1) % NZ)
    seq_r = seq_dev((me_s + 1) % NSEQ)
    seq_l = seq_dev((me_s + NSEQ - 1) % NSEQ)
    x_peer = [seq_dev(((x + j) % NX) * NZ + z) for j in range(1, NX)]
    h_peer = [(me_s, (me_h + j) % NHEAD) for j in range(1, NHEAD)]

    loads = [
        pltpu.make_async_copy(a, b, loc_sem.at[i])
        for i, (a, b) in enumerate(
            ((tk_hbm, tkb), (tv_hbm, tvb), (k_hbm, kraw), (q_hbm, qraw), (v_hbm, vv))
        )
    ]
    for load in loads:
        load.start()

    barrier = pltpu.get_barrier_semaphore()
    peers = [ring_r, ring_l, seq_r, seq_l] + x_peer + h_peer
    for peer in peers:
        pl.semaphore_signal(barrier, inc=1, device_id=peer, device_id_type=MESH)

    def video_of(frame):
        video, first, height, end = jnp.int32(0), jnp.int32(0), shapes_s[1, 0], jnp.int32(0)
        for s in range(SAMPLES - 1):
            count = shapes_s[0, s]
            end = end + count
            past = frame >= end
            video = video + jnp.where(past, 1, 0)
            first = first + jnp.where(past, count, 0)
            height = jnp.where(past, shapes_s[1, s + 1], height)
        return video, frame - first, height

    own_frames = []
    for f in range(2):
        _, time, height = video_of(2 * me_s + f)
        own_frames.append((time, height == 16))

    loads[0].wait()
    loads[1].wait()
    for p in range(SAMPLES):
        o = owner_s[p]
        gat[z, p, 0:PIECE, :] = tkb[o]
        gat[z, p, PIECE : 2 * PIECE, :] = tvb[o]

    pl.semaphore_wait(barrier, len(peers))

    def remote(src, dst, send, recv, dev):
        return pltpu.make_async_remote_copy(
            src_ref=src, dst_ref=dst, send_sem=send, recv_sem=recv, device_id=dev, device_id_type=MESH
        )

    def hop(i):
        right = (z + NZ - (i - 1)) % NZ
        left = (z + (i - 1)) % NZ
        half = SAMPLES // 2
        if i < 4:
            a, b = gat.at[right], gat.at[left]
        else:
            a, b = gat.at[right, pl.ds(0, half)], gat.at[left, pl.ds(half, half)]
        return (
            remote(a, a, g_send.at[0, i - 1], g_recv.at[0, i - 1], ring_r),
            remote(b, b, g_send.at[1, i - 1], g_recv.at[1, i - 1], ring_l),
        )

    hops = {}

    def start_hop(i):
        hops[i] = hop(i)
        for c in hops[i]:
            c.start()

    def end_hop(i):
        for c in hops[i]:
            c.wait_recv()

    start_hop(1)
    v_copies = [
        remote(v_hbm.at[pl.ds(FRAME, FRAME)], vhl.at[0], v_send.at[0], v_recv.at[0], seq_r),
        remote(v_hbm.at[pl.ds(0, FRAME)], vhl.at[1], v_send.at[1], v_recv.at[1], seq_l),
    ]
    for c in v_copies:
        c.start()

    eye = lax.broadcasted_iota(jnp.int32, (TILE, TILE), 0) == lax.broadcasted_iota(
        jnp.int32, (TILE, TILE), 1
    )
    loads[2].wait()
    loads[3].wait()

    def squares(j, carry):
        start = pl.multiple_of(j * TILE, TILE)
        for which, ref in ((0, qraw), (8, kraw)):
            part = jnp.zeros((TILE, HEAD_DIM), F32)
            for h in range(LH):
                w = ref[pl.ds(start, TILE), h * HEAD_DIM : (h + 1) * HEAD_DIM].astype(F32)
                part = part + w * w
            total = jnp.sum(part, axis=1, keepdims=True)
            sums[me_h, pl.ds(which + j, 1), :] = jnp.sum(
                jnp.where(eye, total, 0.0), axis=0, keepdims=True
            )
        return carry

    lax.fori_loop(0, 8, squares, 0)
    s_copies = [
        remote(sums.at[me_h], sums.at[me_h], s_send.at[j], s_recv.at[j], h_peer[j])
        for j in range(NHEAD - 1)
    ]
    for c in s_copies:
        c.start()

    times = lax.broadcasted_iota(jnp.int32, (R_ROW, HEAD_DIM), 0)
    for which, ref in ((0, coss), (1, sins)):
        for j in range(8):
            time, wide = own_frames[j // 4]
            jj = j % 4
            t_row = jnp.sum(
                jnp.where(times == time, tab_ref[which, T_ROW:R_ROW, :], 0.0), axis=0, keepdims=True
            )
            c_rows = tab_ref[which, C_ROW : C_ROW + 16, :]
            if jj % 2:
                c_rows = jnp.where(wide, tab_ref[which, C_ROW + 16 : C_ROW + 32, :], c_rows)
            short, tall = R_ROW + jj // 2 * 8, R_ROW + jj * 8
            r_rows = jnp.where(
                wide, tab_ref[which, short : short + 8, :], tab_ref[which, tall : tall + 8, :]
            )
            r_rows = r_rows + t_row
            for i in range(8):
                ref[j * TILE + i * 16 : j * TILE + (i + 1) * 16, :] = c_rows + r_rows[i : i + 1, :]

    for j in range(8):
        f, jj = j // 4, j % 4
        wide = own_frames[f][1]
        for step in range(3):
            for kk in range(4):
                slot_wide = step * 9 + (kk // 2 - jj // 2 + 1) * 3 + (kk % 2 - jj % 2 + 1)
                entry = win_s[j, slot_wide]
                if abs(kk - jj) <= 1:
                    tall = win_s[j, step * 9 + (kk - jj + 1) * 3 + 1]
                else:
                    tall = jnp.int32(-1)
                entry = jnp.where(wide, entry, tall)
                bias_s[j, (f + step) * 4 + kk] = jnp.where(entry >= 0, F32(0.0), F32(NEG))

    end_hop(1)
    start_hop(2)

    for c in s_copies:
        c.wait_recv()
    total = sums[0]
    for i in range(1, NHEAD):
        total = total + sums[i]
    rk[...] = lax.rsqrt(total / D + EPSILON)

    lane = lax.broadcasted_iota(jnp.int32, (1, HEAD_DIM), 1)
    rowi = lax.broadcasted_iota(jnp.int32, (HEAD_DIM, HEAD_DIM), 0)
    coli = lax.broadcasted_iota(jnp.int32, (HEAD_DIM, HEAD_DIM), 1)
    even = coli % 2 == 0
    swap = (
        jnp.where(even & (rowi == coli + 1), -1.0, 0.0) + jnp.where((~even) & (rowi == coli - 1), 1.0, 0.0)
    ).astype(BF16)

    def rope(raw, gain_ref, which, dst):
        gains = []
        for h in range(LH):
            g = gain_ref[h * HEAD_DIM : (h + 1) * HEAD_DIM].reshape(1, HEAD_DIM)
            gs = jnp.where(
                lane % 2 == 0, pltpu.roll(g, HEAD_DIM - 1, 1), pltpu.roll(g, 1, 1)
            )
            gains.append((g, gs))

        def body(j, carry):
            start = pl.multiple_of(j * TILE, TILE)
            row = rk[pl.ds(which + j, 1), :]
            scale = jnp.sum(jnp.where(eye, row, 0.0), axis=1, keepdims=True)
            cos = coss[pl.ds(start, TILE), :] * scale
            sin = sins[pl.ds(start, TILE), :] * scale
            for h in range(LH):
                w = raw[pl.ds(start, TILE), h * HEAD_DIM : (h + 1) * HEAD_DIM]
                g, gs = gains[h]
                y = w.astype(F32) * g * cos + nn(w, swap) * gs * sin
                dst[h, pl.ds(start, TILE), :] = y.astype(BF16)
            return carry

        lax.fori_loop(0, 8, body, 0)

    rope(kraw, kg_ref, 8, kh)
    k_copies = []
    for h in range(LH):
        k_copies.append(
            (
                remote(kh.at[h, pl.ds(FRAME, FRAME)], khl.at[0, h], k_send.at[0, h], k_recv.at[0, h], seq_r),
                remote(kh.at[h, pl.ds(0, FRAME)], khl.at[1, h], k_send.at[1, h], k_recv.at[1, h], seq_l),
            )
        )
        for c in k_copies[-1]:
            c.start()
    rope(qraw, qg_ref, 0, qh)
    end_hop(2)
    start_hop(3)
    loads[4].wait()

    def columns(h):
        return pl.ds(pl.multiple_of(h * HEAD_DIM, HEAD_DIM), HEAD_DIM)

    QB = 256

    def own_block(h, b, carry):
        start = pl.multiple_of(b * QB, QB)
        s = nt(qh[h, pl.ds(start, QB), :], kh[h])
        v = vv[:, columns(h)]
        parts = []
        for a in range(QB // TILE):
            j = b * (QB // TILE) + a
            sub = [
                s[a * TILE : (a + 1) * TILE, k * TILE : (k + 1) * TILE] + bias_s[j, 4 + k]
                for k in range(8)
            ]
            m = functools.reduce(jnp.maximum, sub)
            m = jnp.broadcast_to(jnp.max(m, axis=1, keepdims=True), (TILE, TILE))
            p = [jnp.exp2((t - m) * SCALE) for t in sub]
            rows = pl.ds(pl.multiple_of(start + a * TILE, TILE), TILE)
            ms[h, rows, :] = m
            ls[h, rows, :] = functools.reduce(jnp.add, p)
            parts.append(jnp.concatenate([t.astype(BF16) for t in p], axis=1))
        acc[h, pl.ds(start, QB), :] = nn(jnp.concatenate(parts, axis=0), v)
        return carry

    def own_head(h):
        lax.fori_loop(0, ROWS // QB, functools.partial(own_block, h), 0)

    def update(h, f, k, v, biased, b, finish):
        start = pl.multiple_of(f * FRAME + b * QB, QB)
        s = nt(qh[h, pl.ds(start, QB), :], k)
        n = k.shape[0] // TILE
        parts, alphas = [], []
        for a in range(QB // TILE):
            j = f * 4 + b * (QB // TILE) + a
            rows = pl.ds(pl.multiple_of(start + a * TILE, TILE), TILE)
            sub = [s[a * TILE : (a + 1) * TILE, i * TILE : (i + 1) * TILE] for i in range(n)]
            if biased is not None:
                sub = [t + bias_s[j, biased + i] for i, t in enumerate(sub)]
            old = ms[h, rows, :]
            m = jnp.max(functools.reduce(jnp.maximum, sub), axis=1, keepdims=True)
            m = jnp.maximum(old, m)
            alpha = jnp.exp2((old - m) * SCALE)
            p = [jnp.exp2((t - m) * SCALE) for t in sub]
            l = functools.reduce(jnp.add, p) + ls[h, rows, :] * alpha
            if finish:
                l = jnp.sum(l, axis=1, keepdims=True)
                parts.append(l)
            else:
                ms[h, rows, :] = m
                ls[h, rows, :] = l
            alphas.append((alpha, jnp.concatenate([t.astype(BF16) for t in p], axis=1)))
        mixed = nn(jnp.concatenate([w for _, w in alphas], axis=0), v)
        for a in range(QB // TILE):
            rows = pl.ds(pl.multiple_of(start + a * TILE, TILE), TILE)
            new = acc[h, rows, :] * alphas[a][0] + mixed[a * TILE : (a + 1) * TILE, :]
            if finish:
                outb[rows, columns(h)] = (new / parts[a]).astype(BF16)
            else:
                acc[h, rows, :] = new

    def own_loop(lo, hi):
        def body(h, carry):
            own_head(h)
            return carry

        lax.fori_loop(lo, hi, body, 0)

    own_loop(0, 1)
    end_hop(3)
    start_hop(4)
    own_loop(1, 2)
    end_hop(4)

    for j in range(NX):
        target = ((x + j) % NX) * NZ + z
        for t in range(2):
            video, _, _ = video_of(2 * target + t)
            for i in range(NZ):
                block = gat[i, video]
                if j == 0:
                    pb[0, t, i] = block
                else:
                    xs[j - 1, t, i] = block
    x_copies = [
        remote(xs.at[j - 1], pb.at[j], x_send.at[j - 1], x_recv.at[j - 1], x_peer[j - 1])
        for j in range(1, NX)
    ]
    for c in x_copies:
        c.start()

    own_loop(2, LH)

    for c in x_copies:
        c.wait_recv()

    def prompt_head(h, carry):
        for f in range(2):
            both = pb[:, f, :, :, columns(h)].reshape(NX * NZ, 2 * PIECE, HEAD_DIM).astype(F32)
            k = both[:, :PIECE, :].reshape(TXT, HEAD_DIM).astype(BF16)
            v = both[:, PIECE:, :].reshape(TXT, HEAD_DIM).astype(BF16)
            for b in range(FRAME // QB):
                update(h, f, k, v, None, b, False)
        return carry

    lax.fori_loop(0, LH, prompt_head, 0)

    for c in v_copies:
        c.wait_recv()
    outs = []
    for h in range(LH):
        for f in range(2):
            k_copies[h][f].wait_recv()
            k = khl[f, h]
            v = vhl[f, :, h * HEAD_DIM : (h + 1) * HEAD_DIM]
            for b in range(FRAME // QB):
                update(h, f, k, v, f * 12, b, True)
        cols = pl.ds(h * HEAD_DIM, HEAD_DIM)
        outs.append(pltpu.make_async_copy(outb.at[:, cols], out_hbm.at[:, cols], out_sem.at[h]))
        outs[-1].start()

    for i in hops:
        for c in hops[i]:
            c.wait_send()
    for c in v_copies + s_copies + x_copies + [c for pair in k_copies for c in pair]:
        c.wait_send()
    for c in outs:
        c.wait()


def local(
    queries, keys, values, query_gain, key_gain, shapes, windows, text_keys, text_values, owner
):
    anyspace = pl.BlockSpec(memory_space=pl.ANY)
    vmem = pl.BlockSpec(memory_space=pltpu.VMEM)
    smem = pl.BlockSpec(memory_space=pltpu.SMEM)
    dma = pltpu.SemaphoreType.DMA
    return pl.pallas_call(
        kernel,
        out_shape=jax.ShapeDtypeStruct((ROWS, WIDTH), BF16),
        in_specs=[anyspace] * 3 + [vmem] * 2 + [smem] * 3 + [anyspace] * 2 + [vmem],
        out_specs=anyspace,
        scratch_shapes=[
            pltpu.VMEM((ROWS, WIDTH), BF16),
            pltpu.VMEM((ROWS, WIDTH), BF16),
            pltpu.VMEM((ROWS, WIDTH), BF16),
            pltpu.VMEM((32, PIECE, WIDTH), BF16),
            pltpu.VMEM((32, PIECE, WIDTH), BF16),
            pltpu.VMEM((LH, ROWS, HEAD_DIM), BF16),
            pltpu.VMEM((LH, ROWS, HEAD_DIM), BF16),
            pltpu.VMEM((2, LH, FRAME, HEAD_DIM), BF16),
            pltpu.VMEM((2, FRAME, WIDTH), BF16),
            pltpu.VMEM((NZ, SAMPLES, 2 * PIECE, WIDTH), BF16),
            pltpu.VMEM((NX - 1, 2, NZ, 2 * PIECE, WIDTH), BF16),
            pltpu.VMEM((NX, 2, NZ, 2 * PIECE, WIDTH), BF16),
            pltpu.VMEM((NHEAD, 16, TILE), F32),
            pltpu.VMEM((ROWS, HEAD_DIM), F32),
            pltpu.VMEM((ROWS, HEAD_DIM), F32),
            pltpu.VMEM((16, TILE), F32),
            pltpu.VMEM((LH, ROWS, HEAD_DIM), F32),
            pltpu.VMEM((LH, ROWS, HEAD_DIM), F32),
            pltpu.VMEM((LH, ROWS, HEAD_DIM), F32),
            pltpu.VMEM((ROWS, WIDTH), BF16),
            pltpu.SMEM((8, 16), F32),
            dma((5,)),
            dma((LH,)),
            dma((2, 4)),
            dma((2, 4)),
            dma((2,)),
            dma((2,)),
            dma((2, LH)),
            dma((2, LH)),
            dma((NHEAD - 1,)),
            dma((NHEAD - 1,)),
            dma((NX - 1,)),
            dma((NX - 1,)),
        ],
        compiler_params=pltpu.CompilerParams(
            collective_id=0, has_side_effects=True, vmem_limit_bytes=56 * 1024 * 1024
        ),
    )(
        queries,
        keys,
        values,
        query_gain,
        key_gain,
        shapes.T,
        windows,
        owner,
        text_keys,
        text_values,
        jnp.asarray(position_tables()),
    )


def solution(mesh):
    placed = (
        P("seq", "head"),
        P("seq", "head"),
        P("seq", "head"),
        P("head"),
        P("head"),
        P(),
        P("seq", None),
        P(None, "seq", "head"),
        P(None, "seq", "head"),
        P(),
    )
    return jax.shard_map(
        local, mesh=mesh, in_specs=placed, out_specs=P("seq", "head"), check_vma=False
    )
```

time: 368 us -> 85.3 us (0.23)
  waiting for transfers between devices: 138 us -> 0 us
  Pallas kernels: 0 us -> 82.6 us
  other arithmetic: 66.5 us -> 0 us
  local copies, waits for them, and re-layouts: 67.2 us -> 2.49 us
  matrix products: 58.5 us -> 0 us
  blocking collectives: 15.2 us -> 0 us
  between operations: 13.6 us -> 0.01 us
  starting transfers between devices: 4.88 us -> 0 us
    pallas_call x0 -> x1, Pallas kernels: none -> 82.6 us  [local(): pl.pallas_call(kernel, out_shape=jax.ShapeDtypeStruct((ROWS, WIDTH), BF16...]
    ppermute x2 -> x0, waiting for transfers between devices: 79.6 us -> none  [the longest x1 68.9 us: extended_2(): lax.ppermute(tail, axis, [(i, (i + 1) % count) for i in range(ends)])]
    dot_general x4 -> x0, matrix products: 58.5 us -> none  [the longest x2 30.4 us: attend(): jnp.einsum('qhd,khd->hqk', query_rows, all_keys, preferred_element_type=j...]
    all_gather x1 -> x0, waiting for transfers between devices: 58.4 us -> none  [local(): every_panel = lax.all_gather(prompt_pair, 'seq', axis=2, tiled=True)]
    reduce_sum x6 -> x0, other arithmetic: 28.6 us -> none  [the longest x2 27.5 us: attend(): totals = jnp.sum(weights, axis=-1)]
    another operation x6 -> x0, other arithmetic: 22.6 us -> none
    psum x1 -> x0, blocking collectives: 15.2 us -> none  [local(): lax.psum((jnp.sum(query_wide * query_wide, axis=1), jnp.sum(key_wide * ke...]
    another operation x4 -> x0, local copies, waits for them, and re-layouts: 11.1 us -> none  [the longest x2 9.08 us: rotate(): field.reshape(field.shape[0], field.shape[1], field.shape[2] // 2, 2)]
  transfers between devices with their start and end apart: 3 -> 0, of which waited for: 3 -> 0; matrix products, arithmetic and copies ran while one was open for 15% -> 0% of each run, Pallas kernels for 0% -> 0%
where the time goes in v1:
time: 85.3 us; the launch traced here: 85.1 us
  Pallas kernels  82.6 us (97%)
  local copies, waits for them, and re-layouts  2.49 us (3%)
    pallas_call x1, Pallas kernels, local(): pl.pallas_call(kernel, out_shape=jax.ShapeDtypeStruct((ROWS, WIDTH), BF16...  82.6 us
    unnamed x1, local copies, waits for them, and re-layouts  2.49 us

profile of v1, /device:TPU:1, one launch (start us, length us, event | category | flops | bytes accessed | tf_op | source)
XLA Modules:
  0.0 85.1 jit_solution(8304658316871886352)
XLA Ops:
  0.0 82.6 %shard_map.109 = bf16[1024,640]{1,0:T(8,128)(2,1)} custom-call(bf16[1024,640]{1,0:T(8,128)(2,1)} %q_hbm.1, bf16[1024,640]{1,0:T(8,128)(2,1)} %k_hbm.1, bf16[1024,640]{1,0:T(8,128)(2,1)} %v_hbm.1, f32[640]{0:T(1024)} %qg_ref.1, f32[640]{0:T(1024)} %kg_ref.1, s32[3,8]{1,0:T(4,128)} %bitcast.1, s32[8,27]{1,0:T(8,128)} %win_s.1, s32[8]{0:T(128)} %owner_s.1, ...), custom_call_target="tpu_custom_call" | custom-call | tf_op jit(solution)/shard_map/pallas_call | solution.py:408
  82.7 2.5 %copy.13 = bf16[1024,640]{1,0:T(8,128)(2,1)} copy(bf16[1024,640]{1,0:T(8,128)(2,1)} %shard_map.109) | data formatting | bytes 2621440

commit v2 on v1

--- a/solution.py
+++ b/solution.py
@@ -56,8 +56,8 @@
 def kernel(
     q_hbm, k_hbm, v_hbm, qg_ref, kg_ref, shapes_s, win_s, owner_s, tk_hbm, tv_hbm, tab_ref,
     out_hbm,
-    qraw, kraw, vv, tkb, tvb, qh, kh, khl, vhl, gat, xs, pb, sums, coss, sins, rk, acc, ms, ls, outb, bias_s,
-    loc_sem, out_sem, g_send, g_recv, v_send, v_recv, k_send, k_recv, s_send, s_recv, x_send, x_recv,
+    qraw, kraw, vv, tkb, tvb, qh, kh, khl, vhl, g0, r1, r2, r3, l1, l2, l3, g4, xs, pb, sums, coss, sins, rk, acc, ms, ls, outb, bias_s,
+    loc_sem, out_sem, g_send, g_recv, v_send, v_recv, p_send, k_send, k_recv, s_send, s_recv, x_send, x_recv,
 ):
     me_s = lax.axis_index("seq")
     me_h = lax.axis_index("head")
@@ -107,8 +107,8 @@
     loads[1].wait()
     for p in range(SAMPLES):
         o = owner_s[p]
-        gat[z, p, 0:PIECE, :] = tkb[o]
-        gat[z, p, PIECE : 2 * PIECE, :] = tvb[o]
+        g0[p, 0:PIECE, :] = tkb[o]
+        g0[p, PIECE : 2 * PIECE, :] = tvb[o]
 
     pl.semaphore_wait(barrier, len(peers))
 
@@ -117,17 +117,19 @@
             src_ref=src, dst_ref=dst, send_sem=send, recv_sem=recv, device_id=dev, device_id_type=MESH
         )
 
+    rights, lefts = (g0, r1, r2, r3), (g0, l1, l2, l3)
+
     def hop(i):
-        right = (z + NZ - (i - 1)) % NZ
-        left = (z + (i - 1)) % NZ
         half = SAMPLES // 2
+        a, b = rights[i - 1], lefts[i - 1]
         if i < 4:
-            a, b = gat.at[right], gat.at[left]
+            c, d = rights[i], lefts[i]
         else:
-            a, b = gat.at[right, pl.ds(0, half)], gat.at[left, pl.ds(half, half)]
+            a, b = a.at[pl.ds(0, half)], b.at[pl.ds(half, half)]
+            c, d = g4.at[pl.ds(0, half)], g4.at[pl.ds(half, half)]
         return (
-            remote(a, a, g_send.at[0, i - 1], g_recv.at[0, i - 1], ring_r),
-            remote(b, b, g_send.at[1, i - 1], g_recv.at[1, i - 1], ring_l),
+            remote(a, c, g_send.at[0, i - 1], g_recv.at[0, i - 1], ring_r),
+            remote(b, d, g_send.at[1, i - 1], g_recv.at[1, i - 1], ring_l),
         )
 
     hops = {}
@@ -141,13 +143,68 @@
         for c in hops[i]:
             c.wait_recv()
 
+    x_videos = [
+        [video_of(2 * (((x + j) % NX) * NZ + z) + t)[0] for t in range(2)] for j in range(NX)
+    ]
+    x_copies = []
+
+    def exchange(i):
+        pieces = ((g0,), (r1, l1), (r2, l2), (r3, l3), (g4,))[i]
+        at = (0, 1, 3, 5, 7)[i]
+        for j in range(NX):
+            for t in range(2):
+                for n, piece in enumerate(pieces):
+                    block = piece[x_videos[j][t]]
+                    if j == 0:
+                        pb[0, at + n, t] = block
+                    else:
+                        xs[j - 1, at + n, t] = block
+        part = pl.ds(at, len(pieces))
+        for j in range(1, NX):
+            c = remote(
+                xs.at[j - 1, part], pb.at[j, part], x_send.at[j - 1, i], x_recv.at[j - 1, i], x_peer[j - 1]
+            )
+            c.start()
+            x_copies.append(c)
+
     start_hop(1)
-    v_copies = [
-        remote(v_hbm.at[pl.ds(FRAME, FRAME)], vhl.at[0], v_send.at[0], v_recv.at[0], seq_r),
-        remote(v_hbm.at[pl.ds(0, FRAME)], vhl.at[1], v_send.at[1], v_recv.at[1], seq_l),
-    ]
-    for c in v_copies:
-        c.start()
+    v_copies = []
+
+    def send_v(i):
+        rows = pl.ds(i * TILE, TILE)
+        for side, first, end, dev, via in (
+            (0, FRAME, NZ - 1, ring_r, x_peer[0]),
+            (1, 0, 0, ring_l, x_peer[NX - 2]),
+        ):
+            slot = jnp.where(z == end, 1, 0)
+            c = remote(
+                v_hbm.at[pl.ds(first + i * TILE, TILE)],
+                vhl.at[side, slot, rows],
+                v_send.at[side, i],
+                v_recv.at[side, slot, i],
+                seq_dev(jnp.where(z == end, via[0], dev[0])),
+            )
+            c.start()
+            v_copies.append(c)
+
+    def passing(side, i):
+        rows = pl.ds(i * TILE, TILE)
+        dev = ring_r if side == 0 else ring_l
+        return remote(
+            vhl.at[side, 1, rows], vhl.at[side, 0, rows], p_send.at[side, i], v_recv.at[side, 0, i], dev
+        )
+
+    def pass_v(i):
+        for side, start in ((0, NZ - 1), (1, 0)):
+
+            @pl.when(z == start)
+            def _():
+                slot = vhl.at[side, 1, pl.ds(i * TILE, TILE)]
+                remote(slot, slot, v_send.at[side, i], v_recv.at[side, 1, i], ring_r).wait_recv()
+                passing(side, i).start()
+
+    send_v(0)
+    exchange(0)
 
     eye = lax.broadcasted_iota(jnp.int32, (TILE, TILE), 0) == lax.broadcasted_iota(
         jnp.int32, (TILE, TILE), 1
@@ -211,6 +268,8 @@
 
     end_hop(1)
     start_hop(2)
+    send_v(1)
+    exchange(1)
 
     for c in s_copies:
         c.wait_recv()
@@ -260,11 +319,12 @@
                 remote(kh.at[h, pl.ds(0, FRAME)], khl.at[1, h], k_send.at[1, h], k_recv.at[1, h], seq_l),
             )
         )
-        for c in k_copies[-1]:
-            c.start()
     rope(qraw, qg_ref, 0, qh)
     end_hop(2)
     start_hop(3)
+    send_v(2)
+    pass_v(0)
+    exchange(2)
     loads[4].wait()
 
     def columns(h):
@@ -339,34 +399,32 @@
     own_loop(0, 1)
     end_hop(3)
     start_hop(4)
+    send_v(3)
+    pass_v(1)
+    exchange(3)
     own_loop(1, 2)
     end_hop(4)
-
-    for j in range(NX):
-        target = ((x + j) % NX) * NZ + z
-        for t in range(2):
-            video, _, _ = video_of(2 * target + t)
-            for i in range(NZ):
-                block = gat[i, video]
-                if j == 0:
-                    pb[0, t, i] = block
-                else:
-                    xs[j - 1, t, i] = block
-    x_copies = [
-        remote(xs.at[j - 1], pb.at[j], x_send.at[j - 1], x_recv.at[j - 1], x_peer[j - 1])
-        for j in range(1, NX)
-    ]
-    for c in x_copies:
-        c.start()
-
-    own_loop(2, LH)
+    exchange(4)
+    pass_v(2)
+
+    def send_k(h):
+        for c in k_copies[h]:
+            c.start()
+
+    send_k(0)
+    send_k(1)
+    for h in range(2, LH):
+        own_loop(h, h + 1)
+        send_k(h)
+        if h == 2:
+            pass_v(3)
 
     for c in x_copies:
         c.wait_recv()
 
     def prompt_head(h, carry):
         for f in range(2):
-            both = pb[:, f, :, :, columns(h)].reshape(NX * NZ, 2 * PIECE, HEAD_DIM).astype(F32)
+            both = pb[:, :, f, :, columns(h)].reshape(NX * NZ, 2 * PIECE, HEAD_DIM).astype(F32)
             k = both[:, :PIECE, :].reshape(TXT, HEAD_DIM).astype(BF16)
             v = both[:, PIECE:, :].reshape(TXT, HEAD_DIM).astype(BF16)
             for b in range(FRAME // QB):
@@ -375,14 +433,16 @@
 
     lax.fori_loop(0, LH, prompt_head, 0)
 
-    for c in v_copies:
-        c.wait_recv()
+    for side in range(2):
+        for i in range(4):
+            rows = vhl.at[side, 0, pl.ds(i * TILE, TILE)]
+            remote(rows, rows, v_send.at[side, i], v_recv.at[side, 0, i], ring_r).wait_recv()
     outs = []
     for h in range(LH):
         for f in range(2):
             k_copies[h][f].wait_recv()
             k = khl[f, h]
-            v = vhl[f, :, h * HEAD_DIM : (h + 1) * HEAD_DIM]
+            v = vhl[f, 0, :, h * HEAD_DIM : (h + 1) * HEAD_DIM]
             for b in range(FRAME // QB):
                 update(h, f, k, v, f * 12, b, True)
         cols = pl.ds(h * HEAD_DIM, HEAD_DIM)
@@ -392,6 +452,13 @@
     for i in hops:
         for c in hops[i]:
             c.wait_send()
+    for side, start in ((0, NZ - 1), (1, 0)):
+
+        @pl.when(z == start)
+        def _():
+            for i in range(4):
+                passing(side, i).wait_send()
+
     for c in v_copies + s_copies + x_copies + [c for pair in k_copies for c in pair]:
         c.wait_send()
     for c in outs:
@@ -401,15 +468,15 @@
 def local(
     queries, keys, values, query_gain, key_gain, shapes, windows, text_keys, text_values, owner
 ):
-    anyspace = pl.BlockSpec(memory_space=pl.ANY)
+    hbm = pl.BlockSpec(memory_space=pltpu.HBM)
     vmem = pl.BlockSpec(memory_space=pltpu.VMEM)
     smem = pl.BlockSpec(memory_space=pltpu.SMEM)
     dma = pltpu.SemaphoreType.DMA
     return pl.pallas_call(
         kernel,
         out_shape=jax.ShapeDtypeStruct((ROWS, WIDTH), BF16),
-        in_specs=[anyspace] * 3 + [vmem] * 2 + [smem] * 3 + [anyspace] * 2 + [vmem],
-        out_specs=anyspace,
+        in_specs=[hbm] * 3 + [vmem] * 2 + [smem] * 3 + [hbm] * 2 + [vmem],
+        out_specs=pl.BlockSpec(memory_space=pl.ANY),
         scratch_shapes=[
             pltpu.VMEM((ROWS, WIDTH), BF16),
             pltpu.VMEM((ROWS, WIDTH), BF16),
@@ -419,10 +486,10 @@
             pltpu.VMEM((LH, ROWS, HEAD_DIM), BF16),
             pltpu.VMEM((LH, ROWS, HEAD_DIM), BF16),
             pltpu.VMEM((2, LH, FRAME, HEAD_DIM), BF16),
-            pltpu.VMEM((2, FRAME, WIDTH), BF16),
-            pltpu.VMEM((NZ, SAMPLES, 2 * PIECE, WIDTH), BF16),
-            pltpu.VMEM((NX - 1, 2, NZ, 2 * PIECE, WIDTH), BF16),
-            pltpu.VMEM((NX, 2, NZ, 2 * PIECE, WIDTH), BF16),
+            pltpu.VMEM((2, 2, FRAME, WIDTH), BF16),
+            *[pltpu.VMEM((SAMPLES, 2 * PIECE, WIDTH), BF16)] * 8,
+            pltpu.VMEM((NX - 1, NZ, 2, 2 * PIECE, WIDTH), BF16),
+            pltpu.VMEM((NX, NZ, 2, 2 * PIECE, WIDTH), BF16),
             pltpu.VMEM((NHEAD, 16, TILE), F32),
             pltpu.VMEM((ROWS, HEAD_DIM), F32),
             pltpu.VMEM((ROWS, HEAD_DIM), F32),
@@ -436,14 +503,15 @@
             dma((LH,)),
             dma((2, 4)),
             dma((2, 4)),
-            dma((2,)),
-            dma((2,)),
+            dma((2, 4)),
+            dma((2, 2, 4)),
+            dma((2, 4)),
             dma((2, LH)),
             dma((2, LH)),
             dma((NHEAD - 1,)),
             dma((NHEAD - 1,)),
-            dma((NX - 1,)),
-            dma((NX - 1,)),
+            dma((NX - 1, 5)),
+            dma((NX - 1, 5)),
         ],
         compiler_params=pltpu.CompilerParams(
             collective_id=0, has_side_effects=True, vmem_limit_bytes=56 * 1024 * 1024

time: 85.3 us -> 64.9 us (0.76)
  Pallas kernels: 82.6 us -> 61.6 us
    pallas_call x1, Pallas kernels: 82.6 us -> 61.6 us  [local(): pl.pallas_call(kernel, out_shape=jax.ShapeDtypeStruct((ROWS, WIDTH), BF16...]
where the time goes in v2:
time: 64.9 us; the launch traced here: 64.1 us
  Pallas kernels  61.6 us (95%)
  local copies, waits for them, and re-layouts  2.49 us (4%)
    pallas_call x1, Pallas kernels, local(): pl.pallas_call(kernel, out_shape=jax.ShapeDtypeStruct((ROWS, WIDTH), BF16...  61.6 us
    unnamed x1, local copies, waits for them, and re-layouts  2.49 us

profile of v2, /device:TPU:1, one launch (start us, length us, event | category | flops | bytes accessed | tf_op | source)
XLA Modules:
  0.0 64.1 jit_solution(15282117385209359539)
XLA Ops:
  0.0 61.6 %shard_map.109 = bf16[1024,640]{1,0:T(8,128)(2,1)} custom-call(bf16[1024,640]{1,0:T(8,128)(2,1)} %q_hbm.1, bf16[1024,640]{1,0:T(8,128)(2,1)} %k_hbm.1, bf16[1024,640]{1,0:T(8,128)(2,1)} %v_hbm.1, f32[640]{0:T(1024)} %qg_ref.1, f32[640]{0:T(1024)} %kg_ref.1, s32[3,8]{1,0:T(4,128)} %bitcast.1, s32[8,27]{1,0:T(8,128)} %win_s.1, s32[8]{0:T(128)} %owner_s.1, ...), custom_call_target="tpu_custom_call" | custom-call | tf_op jit(solution)/shard_map/pallas_call | solution.py:475
  61.7 2.5 %copy.13 = bf16[1024,640]{1,0:T(8,128)(2,1)} copy(bf16[1024,640]{1,0:T(8,128)(2,1)} %shard_map.109) | data formatting | bytes 2621440

commit v3 on v2

--- a/solution.py
+++ b/solution.py
@@ -356,13 +356,15 @@
     def own_head(h):
         lax.fori_loop(0, ROWS // QB, functools.partial(own_block, h), 0)
 
+    HB = 512
+
     def update(h, f, k, v, biased, b, finish):
-        start = pl.multiple_of(f * FRAME + b * QB, QB)
-        s = nt(qh[h, pl.ds(start, QB), :], k)
+        start = pl.multiple_of(f * FRAME + b * HB, HB)
+        s = nt(qh[h, pl.ds(start, HB), :], k)
         n = k.shape[0] // TILE
         parts, alphas = [], []
-        for a in range(QB // TILE):
-            j = f * 4 + b * (QB // TILE) + a
+        for a in range(HB // TILE):
+            j = f * 4 + b * (HB // TILE) + a
             rows = pl.ds(pl.multiple_of(start + a * TILE, TILE), TILE)
             sub = [s[a * TILE : (a + 1) * TILE, i * TILE : (i + 1) * TILE] for i in range(n)]
             if biased is not None:
@@ -381,7 +383,7 @@
                 ls[h, rows, :] = l
             alphas.append((alpha, jnp.concatenate([t.astype(BF16) for t in p], axis=1)))
         mixed = nn(jnp.concatenate([w for _, w in alphas], axis=0), v)
-        for a in range(QB // TILE):
+        for a in range(HB // TILE):
             rows = pl.ds(pl.multiple_of(start + a * TILE, TILE), TILE)
             new = acc[h, rows, :] * alphas[a][0] + mixed[a * TILE : (a + 1) * TILE, :]
             if finish:
@@ -412,22 +414,22 @@
             c.start()
 
     send_k(0)
-    send_k(1)
     for h in range(2, LH):
         own_loop(h, h + 1)
-        send_k(h)
+        send_k(h - 1)
         if h == 2:
             pass_v(3)
 
     for c in x_copies:
         c.wait_recv()
+    send_k(LH - 1)
 
     def prompt_head(h, carry):
         for f in range(2):
             both = pb[:, :, f, :, columns(h)].reshape(NX * NZ, 2 * PIECE, HEAD_DIM).astype(F32)
             k = both[:, :PIECE, :].reshape(TXT, HEAD_DIM).astype(BF16)
             v = both[:, PIECE:, :].reshape(TXT, HEAD_DIM).astype(BF16)
-            for b in range(FRAME // QB):
+            for b in range(FRAME // HB):
                 update(h, f, k, v, None, b, False)
         return carry
 
@@ -443,7 +445,7 @@
             k_copies[h][f].wait_recv()
             k = khl[f, h]
             v = vhl[f, 0, :, h * HEAD_DIM : (h + 1) * HEAD_DIM]
-            for b in range(FRAME // QB):
+            for b in range(FRAME // HB):
                 update(h, f, k, v, f * 12, b, True)
         cols = pl.ds(h * HEAD_DIM, HEAD_DIM)
         outs.append(pltpu.make_async_copy(outb.at[:, cols], out_hbm.at[:, cols], out_sem.at[h]))

time: 64.9 us -> 63.9 us (0.985); the launches traced: 64.1 us -> 63.8 us
  no operation moved by 1% of the time
where the time goes in v3:
time: 63.9 us; the launch traced here: 63.8 us
  Pallas kernels  61.3 us (96%)
  local copies, waits for them, and re-layouts  2.49 us (4%)
    pallas_call x1, Pallas kernels, local(): pl.pallas_call(kernel, out_shape=jax.ShapeDtypeStruct((ROWS, WIDTH), BF16...  61.3 us
    unnamed x1, local copies, waits for them, and re-layouts  2.49 us

profile of v3, /device:TPU:1, one launch (start us, length us, event | category | flops | bytes accessed | tf_op | source)
XLA Modules:
  0.0 63.8 jit_solution(12404950872769246055)
XLA Ops:
  0.0 61.3 %shard_map.109 = bf16[1024,640]{1,0:T(8,128)(2,1)} custom-call(bf16[1024,640]{1,0:T(8,128)(2,1)} %q_hbm.1, bf16[1024,640]{1,0:T(8,128)(2,1)} %k_hbm.1, bf16[1024,640]{1,0:T(8,128)(2,1)} %v_hbm.1, f32[640]{0:T(1024)} %qg_ref.1, f32[640]{0:T(1024)} %kg_ref.1, s32[3,8]{1,0:T(4,128)} %bitcast.1, s32[8,27]{1,0:T(8,128)} %win_s.1, s32[8]{0:T(128)} %owner_s.1, ...), custom_call_target="tpu_custom_call" | custom-call | tf_op jit(solution)/shard_map/pallas_call | solution.py:477
  61.3 2.5 %copy.13 = bf16[1024,640]{1,0:T(8,128)(2,1)} copy(bf16[1024,640]{1,0:T(8,128)(2,1)} %shard_map.109) | data formatting | bytes 2621440

commit v4 on v3

--- a/solution.py
+++ b/solution.py
@@ -319,12 +319,12 @@
                 remote(kh.at[h, pl.ds(0, FRAME)], khl.at[1, h], k_send.at[1, h], k_recv.at[1, h], seq_l),
             )
         )
-    rope(qraw, qg_ref, 0, qh)
     end_hop(2)
     start_hop(3)
     send_v(2)
     pass_v(0)
     exchange(2)
+    rope(qraw, qg_ref, 0, qh)
     loads[4].wait()
 
     def columns(h):

time: 63.9 us -> 63.9 us (level)
  no operation moved by 1% of the time
where the time goes in v4:
time: 63.9 us; the launch traced here: 63.8 us
  Pallas kernels  61.3 us (96%)
  local copies, waits for them, and re-layouts  2.49 us (4%)
    pallas_call x1, Pallas kernels, local(): pl.pallas_call(kernel, out_shape=jax.ShapeDtypeStruct((ROWS, WIDTH), BF16...  61.3 us
    unnamed x1, local copies, waits for them, and re-layouts  2.49 us

profile of v4, /device:TPU:1, one launch (start us, length us, event | category | flops | bytes accessed | tf_op | source)
XLA Modules:
  0.0 63.8 jit_solution(18407458273072430796)
XLA Ops:
  0.0 61.3 %shard_map.109 = bf16[1024,640]{1,0:T(8,128)(2,1)} custom-call(bf16[1024,640]{1,0:T(8,128)(2,1)} %q_hbm.1, bf16[1024,640]{1,0:T(8,128)(2,1)} %k_hbm.1, bf16[1024,640]{1,0:T(8,128)(2,1)} %v_hbm.1, f32[640]{0:T(1024)} %qg_ref.1, f32[640]{0:T(1024)} %kg_ref.1, s32[3,8]{1,0:T(4,128)} %bitcast.1, s32[8,27]{1,0:T(8,128)} %win_s.1, s32[8]{0:T(128)} %owner_s.1, ...), custom_call_target="tpu_custom_call" | custom-call | tf_op jit(solution)/shard_map/pallas_call | solution.py:477
  61.3 2.5 %copy.13 = bf16[1024,640]{1,0:T(8,128)(2,1)} copy(bf16[1024,640]{1,0:T(8,128)(2,1)} %shard_map.109) | data formatting | bytes 2621440
